TPU v7x, 256 devices: a whole 4x4x8 slice. The times are simulated.
256 devices in a mesh: ctx: 32 (over y, x, core), head: 8 (over z).
Axes of the slice: x: 4, y: 4, z: 8, core: 2. Of those that a mesh axis runs over, the one named last changes fastest.
Arguments:
- q_latent: bfloat16 [4096, 128, 512], P('ctx', 'head'), may hold values from -80 to 80
- q_rope: bfloat16 [4096, 8192], P('ctx', 'head'), may hold values from -80 to 80
- kv_latent: bfloat16 [4096, 16, 512], P('ctx', None, 'head'), may hold values from -6.5 to 6.5
- kv_rope: bfloat16 [4096, 1024], P('ctx'), may hold values from -6.5 to 6.5
- grad_out: bfloat16 [4096, 128, 512], P('ctx', 'head'), may hold values from -6 to 6
- block_slot: int32 [4096], replicated, may hold values from 0 to 4095, as said below
- pool: int32 [32, 32, 2], P('ctx'), may hold values from -1 to 4095, as said below
- selected: int32 [4096, 32], P('ctx'), may hold values from 0 to 63, as said below
Outputs:
- d_q_latent: bfloat16 [4096, 128, 512], P('ctx', 'head')
- d_q_rope: bfloat16 [4096, 8192], P('ctx', 'head')
- d_kv_latent: bfloat16 [4096, 16, 512], P('ctx', None, 'head')
- d_kv_rope: bfloat16 [4096, 1024], P('ctx', 'head')
Inputs may be any that keep to these rules, and one draw needn't show every extreme that they name: `block_slot`: a permutation of the context blocks; storage rows r * 128 to (r + 1) * 128 - 1 belong to ctx index r. pool[s, o] lists distinct blocks owned by ctx index o (block_slot // 128 == o) that queries of shard s select, filled slots first, then -1; no block appears twice in pool[s]; each pool[s, o] has 1 or 2 filled slots, and some owner o has all 2 slots filled in pool[s, o] for every s. selected[t] holds 32 distinct positions of filled slots in pool[t // 128] read as 64 slots in a row.
All inputs are finite; a program needn't handle non-finite values.
Results may differ from a plain program's by a relative error of at most 0.0051.
Values may be sent and summed in bfloat16 or wider, within the bound.
A program may use at most 128 MiB of HBM per device.

v0:
```python
import jax
import jax.numpy as jnp
from jax import lax
from jax.sharding import PartitionSpec as P

SCALE = 192.0 ** (-0.5)


def local(q_latent, q_rope, kv_latent, kv_rope, grad_out, block_slot, pool, selected):
    shards = lax.axis_size("ctx")
    owned = kv_latent.shape[0]
    block_len = kv_latent.shape[1]
    cap = pool.shape[2]
    slots = shards * cap
    queries, heads_here, latent = q_latent.shape
    rope = q_rope.shape[1] // heads_here
    wanted = pool[0]
    filled = wanted >= 0
    table = jnp.arange(block_slot.shape[0], dtype=jnp.int32)
    stored = jnp.sum(
        jnp.where(wanted[:, :, None] == table[None, None, :], block_slot[None, None, :], 0), axis=2
    )
    offset = jnp.arange(shards, dtype=jnp.int32)[:, None] * owned
    local_rows = jnp.where(filled, stored - offset, 0)
    requests = lax.all_to_all(local_rows, "ctx", split_axis=0, concat_axis=0, tiled=True)
    full_latent = lax.all_gather(kv_latent, "head", axis=2, tiled=True)
    pool_latent, pool_rope = (
        lax.all_to_all(full_latent[requests], "ctx", split_axis=0, concat_axis=0, tiled=True),
        lax.all_to_all(kv_rope[requests], "ctx", split_axis=0, concat_axis=0, tiled=True),
    )
    width_keys = slots * block_len
    keys_latent = pool_latent.reshape(width_keys, latent)
    keys_rope = pool_rope.reshape(width_keys, rope)
    q_rot = q_rope.reshape(queries, heads_here, rope)
    chosen = jnp.any(
        selected[:, :, None] == jnp.arange(slots, dtype=jnp.int32)[None, None, :], axis=1
    )
    visible = jnp.repeat(chosen, block_len, axis=1)
    step_rows = 64
    count = queries // step_rows

    def one_block(carry, item):
        acc_latent, acc_rope = carry
        q_lat, q_rt, cotan, seen = item
        scores = jnp.einsum("qhl,kl->qhk", q_lat, keys_latent, preferred_element_type=jnp.float32)
        scores = (
            scores + jnp.einsum("qhr,kr->qhk", q_rt, keys_rope, preferred_element_type=jnp.float32)
        ) * SCALE
        scores = jnp.where(seen[:, None, :], scores, -jnp.inf)
        peak = jnp.max(scores, axis=2, keepdims=True)
        weights = jnp.exp(scores - peak)
        probs = weights / jnp.sum(weights, axis=2, keepdims=True)
        dprobs = jnp.einsum("qhl,kl->qhk", cotan, keys_latent, preferred_element_type=jnp.float32)
        delta = jnp.sum(probs * dprobs, axis=2, keepdims=True)
        dscores = (probs * (dprobs - delta) * SCALE).astype(jnp.bfloat16)
        probs_low = probs.astype(jnp.bfloat16)
        grad_qlat = jnp.einsum(
            "qhk,kl->qhl", dscores, keys_latent, preferred_element_type=jnp.float32
        ).astype(jnp.bfloat16)
        grad_qrot = jnp.einsum(
            "qhk,kr->qhr", dscores, keys_rope, preferred_element_type=jnp.float32
        ).astype(jnp.bfloat16)
        acc_latent = acc_latent + jnp.einsum(
            "qhk,qhl->kl", dscores, q_lat, preferred_element_type=jnp.float32
        )
        acc_latent = acc_latent + jnp.einsum(
            "qhk,qhl->kl", probs_low, cotan, preferred_element_type=jnp.float32
        )
        acc_rope = acc_rope + jnp.einsum(
            "qhk,qhr->kr", dscores, q_rt, preferred_element_type=jnp.float32
        )
        return ((acc_latent, acc_rope), (grad_qlat, grad_qrot))

    start = (
        jnp.zeros((width_keys, latent), jnp.float32),
        jnp.zeros((width_keys, rope), jnp.float32),
    )
    items = (
        q_latent.reshape(count, step_rows, heads_here, latent),
        q_rot.reshape(count, step_rows, heads_here, rope),
        grad_out.reshape(count, step_rows, heads_here, latent),
        visible.reshape(count, step_rows, width_keys),
    )
    (grad_latent, grad_rope), (part_qlat, part_qrot) = lax.scan(one_block, start, items)
    d_q_latent = part_qlat.reshape(queries, heads_here, latent)
    d_q_rope = part_qrot.reshape(queries, heads_here * rope)
    grad_latent = grad_latent.reshape(shards, cap, block_len, latent)
    grad_rope = grad_rope.reshape(shards, cap, block_len * rope)
    flat_requests = requests.reshape(slots)
    got_latent, got_rope = (
        lax.all_to_all(grad_latent, "ctx", split_axis=0, concat_axis=0, tiled=True),
        lax.all_to_all(grad_rope, "ctx", split_axis=0, concat_axis=0, tiled=True),
    )
    width = got_latent.shape[3]
    summed_latent = (
        jnp.zeros((owned, block_len, width), jnp.float32)
        .at[flat_requests]
        .add(got_latent.reshape(slots, block_len, width))
    )
    summed_rope = (
        jnp.zeros((owned, got_rope.shape[2]), jnp.float32)
        .at[flat_requests]
        .add(got_rope.reshape(slots, got_rope.shape[2]))
    )
    out_latent, out_rope = (
        lax.psum_scatter(summed_latent, "head", scatter_dimension=2, tiled=True),
        lax.psum_scatter(summed_rope, "head", scatter_dimension=1, tiled=True),
    )
    return (d_q_latent, d_q_rope, out_latent.astype(jnp.bfloat16), out_rope.astype(jnp.bfloat16))


def solution(mesh):
    return jax.shard_map(
        local,
        mesh=mesh,
        in_specs=(
            P("ctx", "head", None),
            P("ctx", "head"),
            P("ctx", None, "head"),
            P("ctx", None),
            P("ctx", "head", None),
            P(),
            P("ctx", None, None),
            P("ctx", None),
        ),
        out_specs=(
            P("ctx", "head", None),
            P("ctx", "head"),
            P("ctx", None, "head"),
            P("ctx", "head"),
        ),
        check_vma=False,
    )
```

profile of v0, /device:TPU:1, one launch (start us, length us, event | category | flops | bytes accessed | tf_op | source)
XLA Modules:
  0.0 346.8 jit_solution(17000684935951401226)
XLA Ops:
  10.9 15.3 %all_to_all.29 = s32[32,1,2]{2,1,0:T(1,128)S(1)} all-to-all(s32[32,1,2]{2,1,0:T(1,128)S(1)} %copy.52), channel_id=1, replica_groups=mesh['ctx'=32,'head'=8] {'ctx'}, dimensions={0} | all-to-all | bytes 512 | tf_op jit(solution)/shard_map/all_to_all | solution.py:25
  28.3 4.2 %all-to-all-start.2 = ((bf16[32,2,1024]{2,1,0:T(2,128)(2,1)}), bf16[32,2,1024]{2,1,0:T(2,128)(2,1)S(1)}, u32[]{:S(2)}, u32[]{:S(2)}) async-start(bf16[32,2,1024]{2,1,0:T(2,128)(2,1)} %reshape.173), calls=%async_computation.2 | async-start | bytes 262144 | tf_op jit(solution)/shard_map/all_to_all | solution.py:29
  32.5 19.2 %all-gather.2.cloned.1.call-done = bf16[128,16,512]{0,1,2:T(8,128)(2,1)} async-done(((bf16[128,16,64]{0,1,2:T(8,128)(2,1)}), bf16[128,16,512]{0,1,2:T(8,128)(2,1)}) %all-gather.2.cloned.1.call-update) | async-done | bytes 2097168 | tf_op jit(solution)/shard_map/all_gather | solution.py:26
  51.6 4.8 %copy.55 = bf16[128,16,512]{2,1,0:T(8,128)(2,1)} copy(bf16[128,16,512]{0,1,2:T(8,128)(2,1)} %all-gather.2.cloned.1.call-done) | data formatting | bytes 4194304 | tf_op jit(solution)/shard_map/all_gather | solution.py:26
  59.8 11.2 %all-to-all-start.1 = ((bf16[32,2,16,512]{3,2,1,0:T(8,128)(2,1)}), bf16[32,2,16,512]{3,2,1,0:T(8,128)(2,1)S(1)}, u32[]{:S(2)}, u32[]{:S(2)}) async-start(bf16[32,2,16,512]{3,2,1,0:T(8,128)(2,1)} %bitcast.115), calls=%async_computation.1 | async-start | bytes 2097152 | tf_op jit(solution)/shard_map/all_to_all | solution.py:28
  80.7 7.5 %all-to-all-done.1 = bf16[32,2,16,512]{3,2,1,0:T(8,128)(2,1)S(1)} async-done(((bf16[32,2,16,512]{3,2,1,0:T(8,128)(2,1)}), bf16[32,2,16,512]{3,2,1,0:T(8,128)(2,1)S(1)}, u32[]{:S(2)}, u32[]{:S(2)}) %all-to-all-start.1) | async-done | bytes 1048608 | tf_op jit(solution)/shard_map/all_to_all | solution.py:28
  88.2 135.3 %while.17 = (s32[]{:T(128)}, f32[1024,512]{1,0:T(8,128)}, f32[1024,64]{0,1:T(8,128)}, bf16[2,64,16,512]{3,2,1,0:T(8,128)(2,1)}, bf16[2,64,16,64]{3,2,1,0:T(8,128...) while((s32[]{:T(128)}, f32[1024,512]{1,0:T(8,128)}, ...), condition=%wide.region_6.7_spmd.clone, body=%wide.region_2.6_spmd.clone.sunk | while | flops 5811416064 | bytes 145199344 | solution.py:84
  95.3 7.3 %fusion.105 = f32[1024,512,1]{1,0,2:T(8,128)} fusion(bf16[2,64,16,512]{3,2,1,0:T(8,128)(2,1)S(1)} %get-tuple-element.280, s32[]{:T(128)S(6)} %copy.68, f32[64,16]{1,0:T(8,128)} %get-tuple-element.242, f32[64,16,1024]{2,1,0:T(8,128)} %copy-done.1), kind=kOutput, calls=%fused_computation.13.clone.1 | convolution fusion | flops 1076889600 | bytes 11567108 | tf_op jit(solution)/shard_map/while/body/eval_jaxpr/qhk,qhl->kl/dot_general | solution.py:66
  105.8 14.2 %bitcast_add_fusion.3 = f32[1024,512]{1,0:T(8,128)} fusion(f32[1024,512,1]{1,0,2:T(8,128)} %fusion.105, f32[1024,512]{1,0:T(8,128)} %get-tuple-element.258, pred[]{:T(512)S(6)} %compare.3, bf16[2,64,16,512]{3,2,1,0:T(8,128)(2,1)} %get-tuple-element.276, s32[]{:T(128)S(6)} %copy.68, f32[64,16,1024]{2,1,0:T(8,128)} %fusion.106, ...), kind=kOutput, calls=%fused_computation.11.clone.1 | convolution fusion | flops 1082656768 | bytes 24182788 | tf_op jit(solution)/shard_map/while/body/eval_jaxpr/qhk,qhl->kl/dot_general | solution.py:63
  120.0 12.3 %fusion.107 = f32[1024,64]{0,1:T(8,128)} fusion(f32[64,16,1024]{2,1,0:T(8,128)} %fusion.106, f32[1024,64]{0,1:T(8,128)} %get-tuple-element.259, bf16[2,64,16,64]{3,2,1,0:T(8,128)(2,1)} %get-tuple-element.278, s32[]{:T(128)S(6)} %copy.68, pred[]{:T(512)S(6)} %compare.3, f32[64,16,1024]{2,1,0:T(8,128)} %get-tuple-element.243, ...), kind=kOutput, calls=%fused_computation.21.clone.1 | convolution fusion | flops 141690880 | bytes 17629188 | tf_op jit(solution)/shard_map/while/body/eval_jaxpr/qhk,qhr->kr/dot_general | solution.py:69
  132.3 11.3 %fusion.108 = bf16[2,64,16,512]{3,2,1,0:T(8,128)(2,1)} fusion(bf16[2,64,16,512]{3,2,1,0:T(8,128)(2,1)} %get-tuple-element.260, s32[]{:T(128)S(6)} %copy.68, bf16[1024,512]{1,0:T(8,128)(2,1)S(1)} %get-tuple-element.277, f32[64,16,1024]{2,1,0:T(8,128)} %fusion.106, f32[64,16,1024]{2,1,0:T(8,128)} %get-tuple-element.243, f32[64,16]{1,0:T(8,128)} %get-tuple-element.242), kind=kOutput, calls=%fused_computation.18.clone.1 | convolution fusion | flops 1081608192 | bytes 18939908 | tf_op jit(solution)/shard_map/while/body/eval_jaxpr/qhk,kl->qhl/dot_general | solution.py:57
  143.7 11.9 %fusion.109 = bf16[2,64,16,64]{3,2,1,0:T(8,128)(2,1)} fusion(bf16[2,64,16,64]{3,2,1,0:T(8,128)(2,1)} %get-tuple-element.261, s32[]{:T(128)S(6)} %copy.68, f32[64,16,1024]{2,1,0:T(8,128)} %fusion.106, bf16[1024,64]{0,1:T(8,128)(2,1)S(1)} %get-tuple-element.279, f32[64,16,1024]{2,1,0:T(8,128)} %get-tuple-element.243, f32[64,16]{1,0:T(8,128)} %get-tuple-element.242), kind=kOutput, calls=%fused_computation.23.clone.1 | convolution fusion | flops 141625344 | bytes 17235972 | tf_op jit(solution)/shard_map/while/body/eval_jaxpr/qhk,kr->qhr/dot_general | solution.py:60
  158.8 3.8 %fusion.104 = (f32[64,16]{1,0:T(8,128)}, f32[64,16,1024]{2,1,0:T(8,128)}) fusion(f32[64,16,1024]{2,1,0:T(8,128)S(1)} %multiply_select_fusion.2), kind=kOutput, calls=%fused_computation.71.clone.1 | output fusion | flops 2098175 | bytes 8392704 | tf_op jit(solution)/shard_map/while/body/eval_jaxpr/sub | solution.py:51
  162.6 7.3 %fusion.105 = f32[1024,512,1]{1,0,2:T(8,128)} fusion(bf16[2,64,16,512]{3,2,1,0:T(8,128)(2,1)S(1)} %get-tuple-element.280, s32[]{:T(128)S(6)} %copy.68, f32[64,16]{1,0:T(8,128)} %get-tuple-element.242, f32[64,16,1024]{2,1,0:T(8,128)} %copy-done.1), kind=kOutput, calls=%fused_computation.13.clone.1 | convolution fusion | flops 1076889600 | bytes 11567108 | tf_op jit(solution)/shard_map/while/body/eval_jaxpr/qhk,qhl->kl/dot_general | solution.py:66
  173.2 14.8 %bitcast_add_fusion.3 = f32[1024,512]{1,0:T(8,128)} fusion(f32[1024,512,1]{1,0,2:T(8,128)} %fusion.105, f32[1024,512]{1,0:T(8,128)} %get-tuple-element.258, pred[]{:T(512)S(6)} %compare.3, bf16[2,64,16,512]{3,2,1,0:T(8,128)(2,1)} %get-tuple-element.276, s32[]{:T(128)S(6)} %copy.68, f32[64,16,1024]{2,1,0:T(8,128)} %fusion.106, ...), kind=kOutput, calls=%fused_computation.11.clone.1 | convolution fusion | flops 1082656768 | bytes 24182788 | tf_op jit(solution)/shard_map/while/body/eval_jaxpr/qhk,qhl->kl/dot_general | solution.py:63
  187.9 12.3 %fusion.107 = f32[1024,64]{0,1:T(8,128)} fusion(f32[64,16,1024]{2,1,0:T(8,128)} %fusion.106, f32[1024,64]{0,1:T(8,128)} %get-tuple-element.259, bf16[2,64,16,64]{3,2,1,0:T(8,128)(2,1)} %get-tuple-element.278, s32[]{:T(128)S(6)} %copy.68, pred[]{:T(512)S(6)} %compare.3, f32[64,16,1024]{2,1,0:T(8,128)} %get-tuple-element.243, ...), kind=kOutput, calls=%fused_computation.21.clone.1 | convolution fusion | flops 141690880 | bytes 17629188 | tf_op jit(solution)/shard_map/while/body/eval_jaxpr/qhk,qhr->kr/dot_general | solution.py:69
  200.3 11.3 %fusion.108 = bf16[2,64,16,512]{3,2,1,0:T(8,128)(2,1)} fusion(bf16[2,64,16,512]{3,2,1,0:T(8,128)(2,1)} %get-tuple-element.260, s32[]{:T(128)S(6)} %copy.68, bf16[1024,512]{1,0:T(8,128)(2,1)S(1)} %get-tuple-element.277, f32[64,16,1024]{2,1,0:T(8,128)} %fusion.106, f32[64,16,1024]{2,1,0:T(8,128)} %get-tuple-element.243, f32[64,16]{1,0:T(8,128)} %get-tuple-element.242), kind=kOutput, calls=%fused_computation.18.clone.1 | convolution fusion | flops 1081608192 | bytes 18939908 | tf_op jit(solution)/shard_map/while/body/eval_jaxpr/qhk,kl->qhl/dot_general | solution.py:57
  211.6 11.9 %fusion.109 = bf16[2,64,16,64]{3,2,1,0:T(8,128)(2,1)} fusion(bf16[2,64,16,64]{3,2,1,0:T(8,128)(2,1)} %get-tuple-element.261, s32[]{:T(128)S(6)} %copy.68, f32[64,16,1024]{2,1,0:T(8,128)} %fusion.106, bf16[1024,64]{0,1:T(8,128)(2,1)S(1)} %get-tuple-element.279, f32[64,16,1024]{2,1,0:T(8,128)} %get-tuple-element.243, f32[64,16]{1,0:T(8,128)} %get-tuple-element.242), kind=kOutput, calls=%fused_computation.23.clone.1 | convolution fusion | flops 141625344 | bytes 17235972 | tf_op jit(solution)/shard_map/while/body/eval_jaxpr/qhk,kr->qhr/dot_general | solution.py:60
  224.9 12.4 %all_to_all.30 = f32[32,2,1024]{2,1,0:T(2,128)S(1)} all-to-all(f32[32,2,1024]{2,1,0:T(2,128)S(1)} %reshape.162), channel_id=1, replica_groups=mesh['ctx'=32,'head'=8] {'ctx'}, dimensions={0} | all-to-all | bytes 524288 | tf_op jit(solution)/shard_map/all_to_all | solution.py:92
  237.3 3.9 %all-to-all-start.3 = ((f32[32,2,16,512]{3,2,1,0:T(8,128)}), f32[32,2,16,512]{3,2,1,0:T(8,128)S(1)}, u32[]{:S(2)}, u32[]{:S(2)}) async-start(f32[32,2,16,512]{3,2,1,0:T(8,128)} %bitcast.116), calls=%async_computation.3 | async-start | bytes 4194304 | tf_op jit(solution)/shard_map/all_to_all | solution.py:91
  244.8 24.4 %all-to-all-done.3 = f32[32,2,16,512]{3,2,1,0:T(8,128)S(1)} async-done(((f32[32,2,16,512]{3,2,1,0:T(8,128)}), f32[32,2,16,512]{3,2,1,0:T(8,128)S(1)}, u32[]{:S(2)}, u32[]{:S(2)}) %all-to-all-start.3) | async-done | bytes 2097184 | tf_op jit(solution)/shard_map/all_to_all | solution.py:91
  271.7 9.0 %scatter_fusion = f32[128,16,512]{2,1,0:T(8,128)} fusion(f32[128,16,512]{2,1,0:T(8,128)} %broadcast_in_dim.77, s32[64]{0:T(128)S(1)} %fusion.56, f32[64,16,512]{2,1,0:T(8,128)S(1)} %bitcast.114), kind=kCustom, calls=%fused_computation.2 | custom fusion | flops 524288 | bytes 6291712 | tf_op jit(solution)/shard_map/scatter-add | solution.py:98
  280.7 5.8 %copy.58 = f32[128,16,512]{0,1,2:T(8,128)} copy(f32[128,16,512]{2,1,0:T(8,128)} %scatter_fusion) | data formatting | bytes 8388608 | tf_op jit(solution)/shard_map/scatter-add | solution.py:98
  290.1 48.3 %reduce-scatter.3.cloned.1.call-done = f32[128,16,64]{0,1,2:T(8,128)} async-done(((f32[128,16,512]{0,1,2:T(8,128)}), f32[128,16,64]{0,1,2:T(8,128)}) %reduce-scatter.3.cloned.1.call-update) | async-done | bytes 524304 | tf_op jit(solution)/shard_map/reduce_scatter | solution.py:106
  (78 shorter events, 48.3 us)
Async XLA Ops:
  7.2 19.7 %copy-start = (bf16[128,1024]{1,0:T(8,128)(2,1)S(1)}, bf16[128,1024]{1,0:T(8,128)(2,1)}, u32[]{:S(2)}) copy-start(bf16[128,1024]{1,0:T(8,128)(2,1)} %param.13) | copy-start | bytes 786436
  7.2 44.4 %all-gather.2.cloned.1.call-start = ((), (), s32[]{:S(2)}) async-start(), calls=%async_computation.7 | async-start | bytes 2359296 | tf_op jit(solution)/shard_map/all_gather | solution.py:26
  26.2 0.6 copy-start.6
  28.3 31.5 %all-to-all-start.2 = ((bf16[32,2,1024]{2,1,0:T(2,128)(2,1)}), bf16[32,2,1024]{2,1,0:T(2,128)(2,1)S(1)}, u32[]{:S(2)}, u32[]{:S(2)}) async-start(bf16[32,2,1024]{2,1,0:T(2,128)(2,1)} %reshape.173), calls=%async_computation.2 | async-start | bytes 262144 | tf_op jit(solution)/shard_map/all_to_all | solution.py:29
  32.4 38.6 %copy-start.8 = (s32[128,32]{0,1:T(8,128)S(1)}, s32[128,32]{0,1:T(8,128)}, u32[]{:S(2)}) copy-start(s32[128,32]{0,1:T(8,128)} %param.17) | copy-start | bytes 49156
  56.4 31.8 %copy-start.2 = (bf16[128,16,512]{2,1,0:T(8,128)(2,1)S(1)}, bf16[128,16,512]{2,1,0:T(8,128)(2,1)}, u32[]{:S(2)}) copy-start(bf16[128,16,512]{2,1,0:T(8,128)(2,1)} %param.14) | copy-start | bytes 6291460
  59.8 28.4 %all-to-all-start.1 = ((bf16[32,2,16,512]{3,2,1,0:T(8,128)(2,1)}), bf16[32,2,16,512]{3,2,1,0:T(8,128)(2,1)S(1)}, u32[]{:S(2)}, u32[]{:S(2)}) async-start(bf16[32,2,16,512]{3,2,1,0:T(8,128)(2,1)} %bitcast.115), calls=%async_computation.1 | async-start | bytes 2097152 | tf_op jit(solution)/shard_map/all_to_all | solution.py:28
  88.2 1.8 copy-start.4
  88.2 1.8 copy-start.3
  91.5 3.8 %copy-start.1 = (f32[64,16,1024]{2,1,0:T(8,128)}, f32[64,16,1024]{2,1,0:T(8,128)S(1)}, u32[]{:S(2)}) copy-start(f32[64,16,1024]{2,1,0:T(8,128)S(1)} %multiply_select_fusion.2) | copy-start | bytes 12582916 | tf_op jit(solution)/shard_map/while
  155.5 1.8 copy-start.4
  155.6 1.8 copy-start.3
  158.8 3.8 %copy-start.1 = (f32[64,16,1024]{2,1,0:T(8,128)}, f32[64,16,1024]{2,1,0:T(8,128)S(1)}, u32[]{:S(2)}) copy-start(f32[64,16,1024]{2,1,0:T(8,128)S(1)} %multiply_select_fusion.2) | copy-start | bytes 12582916 | tf_op jit(solution)/shard_map/while
  223.5 18.3 %copy-start.7 = (s32[32,1,2]{2,1,0:T(1,128)S(1)}, s32[32,1,2]{2,1,0:T(1,128)}, u32[]{:S(2)}) copy-start(s32[32,1,2]{2,1,0:T(1,128)} %copy-done.6) | copy-start | bytes 772
  237.3 31.9 %all-to-all-start.3 = ((f32[32,2,16,512]{3,2,1,0:T(8,128)}), f32[32,2,16,512]{3,2,1,0:T(8,128)S(1)}, u32[]{:S(2)}, u32[]{:S(2)}) async-start(f32[32,2,16,512]{3,2,1,0:T(8,128)} %bitcast.116), calls=%async_computation.3 | async-start | bytes 4194304 | tf_op jit(solution)/shard_map/all_to_all | solution.py:91
  241.2 47.4 %reduce-scatter.5.cloned.1.call-start = ((), (), s32[]{:S(2)}) async-start(), calls=%async_computation.9 | async-start | bytes 589824 | tf_op jit(solution)/shard_map/reduce_scatter | solution.py:107
  244.7 93.6 %reduce-scatter.3.cloned.1.call-start = ((), (), s32[]{:S(2)}) async-start(), calls=%async_computation.8 | async-start | bytes 4718592 | tf_op jit(solution)/shard_map/reduce_scatter | solution.py:106
  286.6 1.0 copy-start.5
Sparse Core Ops, SparseCore 0:
  10.4 41.1 all-gather.1
  244.9 31.8 reduce-scatter.4
  286.7 51.6 reduce-scatter.2
where the time goes:
time: 348 us; the launch traced here: 347 us
  matrix products  128 us (37%)
  waiting for transfers between devices  99.3 us (29%)
  local copies, waits for them, and re-layouts  35.1 us (10%)
  blocking collectives  27.7 us (8%)
  other arithmetic  23.6 us (7%)
  starting transfers between devices  19.4 us (6%)
  between operations  13.9 us (4%)
    reduce_scatter x1, waiting for transfers between devices, local(): lax.psum_scatter(summed_latent, 'head', scatter_dimension=2, tiled=True)  48.3 us
    dot_general x2, matrix products, one_block(): jnp.einsum('qhk,qhl->kl', dscores, q_lat, preferred_element_type=jnp.floa...  28.9 us
    dot_general x2, matrix products, one_block(): jnp.einsum('qhk,qhr->kr', dscores, q_rt, preferred_element_type=jnp.float32)  24.7 us
    all_to_all x1, waiting for transfers between devices, local(): lax.all_to_all(grad_latent, 'ctx', split_axis=0, concat_axis=0, tiled=True)  24.4 us
    dot_general x2, matrix products, one_block(): jnp.einsum('qhk,kr->qhr', dscores, keys_rope, preferred_element_type=jnp....  23.7 us
    dot_general x2, matrix products, one_block(): jnp.einsum('qhk,kl->qhl', dscores, keys_latent, preferred_element_type=jn...  22.7 us
    all_gather x1, waiting for transfers between devices, local(): full_latent = lax.all_gather(kv_latent, 'head', axis=2, tiled=True)  19.2 us
    all_to_all x1, blocking collectives, local(): lax.all_to_all(local_rows, 'ctx', split_axis=0, concat_axis=0, tiled=True)  15.3 us
  transfers between devices with their start and end apart: 6, of which 4 were waited for; matrix products, arithmetic and copies ran while one was open for 13% of the time, Pallas kernels for 0%

commit v1 on v0

--- a/solution.py
+++ b/solution.py
@@ -4,6 +4,11 @@
 from jax.sharding import PartitionSpec as P
 
 SCALE = 192.0 ** (-0.5)
+
+
+def swapped_in(value, axis, dim):
+    sent = jnp.stack([value] * lax.axis_size(axis))
+    return jnp.concatenate(lax.all_to_all(sent, axis, 0, 0), axis=dim)
 
 
 def local(q_latent, q_rope, kv_latent, kv_rope, grad_out, block_slot, pool, selected):
@@ -23,7 +28,7 @@
     offset = jnp.arange(shards, dtype=jnp.int32)[:, None] * owned
     local_rows = jnp.where(filled, stored - offset, 0)
     requests = lax.all_to_all(local_rows, "ctx", split_axis=0, concat_axis=0, tiled=True)
-    full_latent = lax.all_gather(kv_latent, "head", axis=2, tiled=True)
+    full_latent = swapped_in(kv_latent, "head", 2)
     pool_latent, pool_rope = (
         lax.all_to_all(full_latent[requests], "ctx", split_axis=0, concat_axis=0, tiled=True),
         lax.all_to_all(kv_rope[requests], "ctx", split_axis=0, concat_axis=0, tiled=True),

time: 348 us -> 383 us (1.10)
  waiting for transfers between devices: 99.3 us -> 124 us
  starting transfers between devices: 19.4 us -> 26.9 us
    all_to_all x0 -> x1, waiting for transfers between devices: none -> 46.7 us  [swapped_in(): return jnp.concatenate(lax.all_to_all(sent, axis, 0, 0), axis=dim)]
    all_gather x1 -> x0, waiting for transfers between devices: 19.2 us -> none  [local(): full_latent = lax.all_gather(kv_latent, 'head', axis=2, tiled=True)]
    all_to_all x0 -> x1, starting transfers between devices: none -> 8.19 us  [swapped_in(): return jnp.concatenate(lax.all_to_all(sent, axis, 0, 0), axis=dim)]
    all_gather x1 -> x0, local copies, waits for them, and re-layouts: 4.82 us -> none  [local(): full_latent = lax.all_gather(kv_latent, 'head', axis=2, tiled=True)]
    reshape x0 -> x1, local copies, waits for them, and re-layouts: none -> 4.63 us  [swapped_in(): return jnp.concatenate(lax.all_to_all(sent, axis, 0, 0), axis=dim)]
  transfers between devices with their start and end apart: 6 -> 6, of which waited for: 4 -> 4; matrix products, arithmetic and copies ran while one was open for 13% -> 12% of each run, Pallas kernels for 0% -> 0%
where the time goes in v1:
time: 383 us; the launch traced here: 382 us
  matrix products  128 us (33%)
  waiting for transfers between devices  124 us (32%)
  local copies, waits for them, and re-layouts  37.1 us (10%)
  blocking collectives  27.7 us (7%)
  starting transfers between devices  26.9 us (7%)
  other arithmetic  24.3 us (6%)
  between operations  14.2 us (4%)
    all_to_all x1, waiting for transfers between devices, swapped_in(): return jnp.concatenate(lax.all_to_all(sent, axis, 0, 0), axis=dim)  46.7 us
    reduce_scatter x1, waiting for transfers between devices, local(): lax.psum_scatter(summed_latent, 'head', scatter_dimension=2, tiled=True)  45.7 us
    dot_general x2, matrix products, one_block(): jnp.einsum('qhk,qhl->kl', dscores, q_lat, preferred_element_type=jnp.floa...  28.9 us
    dot_general x2, matrix products, one_block(): jnp.einsum('qhk,qhr->kr', dscores, q_rt, preferred_element_type=jnp.float32)  24.7 us
    all_to_all x1, waiting for transfers between devices, local(): lax.all_to_all(grad_latent, 'ctx', split_axis=0, concat_axis=0, tiled=True)  24.4 us
    dot_general x2, matrix products, one_block(): jnp.einsum('qhk,kr->qhr', dscores, keys_rope, preferred_element_type=jnp....  23.7 us
    dot_general x2, matrix products, one_block(): jnp.einsum('qhk,kl->qhl', dscores, keys_latent, preferred_element_type=jn...  22.7 us
    all_to_all x1, blocking collectives, local(): lax.all_to_all(local_rows, 'ctx', split_axis=0, concat_axis=0, tiled=True)  15.3 us
  transfers between devices with their start and end apart: 6, of which 4 were waited for; matrix products, arithmetic and copies ran while one was open for 12% of the time, Pallas kernels for 0%

profile of v1, /device:TPU:1, one launch (start us, length us, event | category | flops | bytes accessed | tf_op | source)
XLA Modules:
  0.0 381.5 jit_solution(14899378028248105288)
XLA Ops:
  9.0 15.3 %all_to_all.34 = s32[32,1,2]{2,1,0:T(1,128)S(1)} all-to-all(s32[32,1,2]{2,1,0:T(1,128)S(1)} %copy.61), channel_id=1, replica_groups=mesh['ctx'=32,'head'=8] {'ctx'}, dimensions={0} | all-to-all | bytes 512 | tf_op jit(solution)/shard_map/all_to_all | solution.py:30
  27.2 8.2 %all-to-all-start = ((bf16[8,128,16,64]{1,3,2,0:T(8,128)(2,1)}), bf16[8,128,16,64]{1,3,2,0:T(8,128)(2,1)S(1)}, u32[]{:S(2)}, u32[]{:S(2)}) async-start(bf16[8,128,16,64]{1,3,2,0:T(8,128)(2,1)} %stack.2), calls=%async_computation | async-start | bytes 4194304 | tf_op jit(solution)/shard_map/all_to_all | solution.py:11
  37.1 46.7 %all-to-all-done = bf16[8,128,16,64]{1,3,2,0:T(8,128)(2,1)S(1)} async-done(((bf16[8,128,16,64]{1,3,2,0:T(8,128)(2,1)}), bf16[8,128,16,64]{1,3,2,0:T(8,128)(2,1)S(1)}, u32[]{:S(2)}, u32[]{:S(2)}) %all-to-all-start) | async-done | bytes 2097184 | tf_op jit(solution)/shard_map/all_to_all | solution.py:11
  83.8 7.2 %all-to-all-start.3 = ((bf16[32,2,1024]{2,1,0:T(2,128)(2,1)}), bf16[32,2,1024]{2,1,0:T(2,128)(2,1)S(1)}, u32[]{:S(2)}, u32[]{:S(2)}) async-start(bf16[32,2,1024]{2,1,0:T(2,128)(2,1)} %reshape.183), calls=%async_computation.3 | async-start | bytes 262144 | tf_op jit(solution)/shard_map/all_to_all | solution.py:34
  92.6 4.6 %copy.64 = bf16[128,16,512]{2,1,0:T(8,128)(2,1)} copy(bf16[128,16,512]{0,2,1:T(8,128)(2,1)} %bitcast.118) | data formatting | bytes 4194304 | tf_op jit(solution)/shard_map/reshape | solution.py:11
  100.6 7.5 %all-to-all-start.2 = ((bf16[32,2,16,512]{3,2,1,0:T(8,128)(2,1)}), bf16[32,2,16,512]{3,2,1,0:T(8,128)(2,1)S(1)}, u32[]{:S(2)}, u32[]{:S(2)}) async-start(bf16[32,2,16,512]{3,2,1,0:T(8,128)(2,1)} %bitcast.119), calls=%async_computation.2 | async-start | bytes 2097152 | tf_op jit(solution)/shard_map/all_to_all | solution.py:33
  118.5 6.7 %all-to-all-done.2 = bf16[32,2,16,512]{3,2,1,0:T(8,128)(2,1)S(1)} async-done(((bf16[32,2,16,512]{3,2,1,0:T(8,128)(2,1)}), bf16[32,2,16,512]{3,2,1,0:T(8,128)(2,1)S(1)}, u32[]{:S(2)}, u32[]{:S(2)}) %all-to-all-start.2) | async-done | bytes 1048608 | tf_op jit(solution)/shard_map/all_to_all | solution.py:33
  125.2 135.3 %while.17 = (s32[]{:T(128)}, f32[1024,512]{1,0:T(8,128)}, f32[1024,64]{0,1:T(8,128)}, bf16[2,64,16,512]{3,2,1,0:T(8,128)(2,1)}, bf16[2,64,16,64]{3,2,1,0:T(8,128...) while((s32[]{:T(128)}, f32[1024,512]{1,0:T(8,128)}, ...), condition=%wide.region_6.7_spmd.clone, body=%wide.region_2.6_spmd.clone.sunk | while | flops 5811416064 | bytes 145199344 | solution.py:89
  132.3 7.3 %fusion.105 = f32[1024,512,1]{1,0,2:T(8,128)} fusion(bf16[2,64,16,512]{3,2,1,0:T(8,128)(2,1)S(1)} %get-tuple-element.295, s32[]{:T(128)S(6)} %copy.77, f32[64,16]{1,0:T(8,128)} %get-tuple-element.257, f32[64,16,1024]{2,1,0:T(8,128)} %copy-done.1), kind=kOutput, calls=%fused_computation.13.clone.1 | convolution fusion | flops 1076889600 | bytes 11567108 | tf_op jit(solution)/shard_map/while/body/eval_jaxpr/qhk,qhl->kl/dot_general | solution.py:71
  142.9 14.2 %bitcast_add_fusion.3 = f32[1024,512]{1,0:T(8,128)} fusion(f32[1024,512,1]{1,0,2:T(8,128)} %fusion.105, f32[1024,512]{1,0:T(8,128)} %get-tuple-element.273, pred[]{:T(512)S(6)} %compare.3, bf16[2,64,16,512]{3,2,1,0:T(8,128)(2,1)} %get-tuple-element.291, s32[]{:T(128)S(6)} %copy.77, f32[64,16,1024]{2,1,0:T(8,128)} %fusion.106, ...), kind=kOutput, calls=%fused_computation.11.clone.1 | convolution fusion | flops 1082656768 | bytes 24182788 | tf_op jit(solution)/shard_map/while/body/eval_jaxpr/qhk,qhl->kl/dot_general | solution.py:68
  157.0 12.3 %fusion.107 = f32[1024,64]{0,1:T(8,128)} fusion(f32[64,16,1024]{2,1,0:T(8,128)} %fusion.106, f32[1024,64]{0,1:T(8,128)} %get-tuple-element.274, bf16[2,64,16,64]{3,2,1,0:T(8,128)(2,1)} %get-tuple-element.293, s32[]{:T(128)S(6)} %copy.77, pred[]{:T(512)S(6)} %compare.3, f32[64,16,1024]{2,1,0:T(8,128)} %get-tuple-element.258, ...), kind=kOutput, calls=%fused_computation.21.clone.1 | convolution fusion | flops 141690880 | bytes 17629188 | tf_op jit(solution)/shard_map/while/body/eval_jaxpr/qhk,qhr->kr/dot_general | solution.py:74
  169.4 11.3 %fusion.108 = bf16[2,64,16,512]{3,2,1,0:T(8,128)(2,1)} fusion(bf16[2,64,16,512]{3,2,1,0:T(8,128)(2,1)} %get-tuple-element.275, s32[]{:T(128)S(6)} %copy.77, bf16[1024,512]{1,0:T(8,128)(2,1)S(1)} %get-tuple-element.292, f32[64,16,1024]{2,1,0:T(8,128)} %fusion.106, f32[64,16,1024]{2,1,0:T(8,128)} %get-tuple-element.258, f32[64,16]{1,0:T(8,128)} %get-tuple-element.257), kind=kOutput, calls=%fused_computation.18.clone.1 | convolution fusion | flops 1081608192 | bytes 18939908 | tf_op jit(solution)/shard_map/while/body/eval_jaxpr/qhk,kl->qhl/dot_general | solution.py:62
  180.7 11.9 %fusion.109 = bf16[2,64,16,64]{3,2,1,0:T(8,128)(2,1)} fusion(bf16[2,64,16,64]{3,2,1,0:T(8,128)(2,1)} %get-tuple-element.276, s32[]{:T(128)S(6)} %copy.77, f32[64,16,1024]{2,1,0:T(8,128)} %fusion.106, bf16[1024,64]{0,1:T(8,128)(2,1)S(1)} %get-tuple-element.294, f32[64,16,1024]{2,1,0:T(8,128)} %get-tuple-element.258, f32[64,16]{1,0:T(8,128)} %get-tuple-element.257), kind=kOutput, calls=%fused_computation.23.clone.1 | convolution fusion | flops 141625344 | bytes 17235972 | tf_op jit(solution)/shard_map/while/body/eval_jaxpr/qhk,kr->qhr/dot_general | solution.py:65
  199.6 7.3 %fusion.105 = f32[1024,512,1]{1,0,2:T(8,128)} fusion(bf16[2,64,16,512]{3,2,1,0:T(8,128)(2,1)S(1)} %get-tuple-element.295, s32[]{:T(128)S(6)} %copy.77, f32[64,16]{1,0:T(8,128)} %get-tuple-element.257, f32[64,16,1024]{2,1,0:T(8,128)} %copy-done.1), kind=kOutput, calls=%fused_computation.13.clone.1 | convolution fusion | flops 1076889600 | bytes 11567108 | tf_op jit(solution)/shard_map/while/body/eval_jaxpr/qhk,qhl->kl/dot_general | solution.py:71
  210.2 14.8 %bitcast_add_fusion.3 = f32[1024,512]{1,0:T(8,128)} fusion(f32[1024,512,1]{1,0,2:T(8,128)} %fusion.105, f32[1024,512]{1,0:T(8,128)} %get-tuple-element.273, pred[]{:T(512)S(6)} %compare.3, bf16[2,64,16,512]{3,2,1,0:T(8,128)(2,1)} %get-tuple-element.291, s32[]{:T(128)S(6)} %copy.77, f32[64,16,1024]{2,1,0:T(8,128)} %fusion.106, ...), kind=kOutput, calls=%fused_computation.11.clone.1 | convolution fusion | flops 1082656768 | bytes 24182788 | tf_op jit(solution)/shard_map/while/body/eval_jaxpr/qhk,qhl->kl/dot_general | solution.py:68
  225.0 12.3 %fusion.107 = f32[1024,64]{0,1:T(8,128)} fusion(f32[64,16,1024]{2,1,0:T(8,128)} %fusion.106, f32[1024,64]{0,1:T(8,128)} %get-tuple-element.274, bf16[2,64,16,64]{3,2,1,0:T(8,128)(2,1)} %get-tuple-element.293, s32[]{:T(128)S(6)} %copy.77, pred[]{:T(512)S(6)} %compare.3, f32[64,16,1024]{2,1,0:T(8,128)} %get-tuple-element.258, ...), kind=kOutput, calls=%fused_computation.21.clone.1 | convolution fusion | flops 141690880 | bytes 17629188 | tf_op jit(solution)/shard_map/while/body/eval_jaxpr/qhk,qhr->kr/dot_general | solution.py:74
  237.3 11.3 %fusion.108 = bf16[2,64,16,512]{3,2,1,0:T(8,128)(2,1)} fusion(bf16[2,64,16,512]{3,2,1,0:T(8,128)(2,1)} %get-tuple-element.275, s32[]{:T(128)S(6)} %copy.77, bf16[1024,512]{1,0:T(8,128)(2,1)S(1)} %get-tuple-element.292, f32[64,16,1024]{2,1,0:T(8,128)} %fusion.106, f32[64,16,1024]{2,1,0:T(8,128)} %get-tuple-element.258, f32[64,16]{1,0:T(8,128)} %get-tuple-element.257), kind=kOutput, calls=%fused_computation.18.clone.1 | convolution fusion | flops 1081608192 | bytes 18939908 | tf_op jit(solution)/shard_map/while/body/eval_jaxpr/qhk,kl->qhl/dot_general | solution.py:62
  248.6 11.9 %fusion.109 = bf16[2,64,16,64]{3,2,1,0:T(8,128)(2,1)} fusion(bf16[2,64,16,64]{3,2,1,0:T(8,128)(2,1)} %get-tuple-element.276, s32[]{:T(128)S(6)} %copy.77, f32[64,16,1024]{2,1,0:T(8,128)} %fusion.106, bf16[1024,64]{0,1:T(8,128)(2,1)S(1)} %get-tuple-element.294, f32[64,16,1024]{2,1,0:T(8,128)} %get-tuple-element.258, f32[64,16]{1,0:T(8,128)} %get-tuple-element.257), kind=kOutput, calls=%fused_computation.23.clone.1 | convolution fusion | flops 141625344 | bytes 17235972 | tf_op jit(solution)/shard_map/while/body/eval_jaxpr/qhk,kr->qhr/dot_general | solution.py:65
  261.9 12.4 %all_to_all.35 = f32[32,2,1024]{2,1,0:T(2,128)S(1)} all-to-all(f32[32,2,1024]{2,1,0:T(2,128)S(1)} %reshape.172), channel_id=1, replica_groups=mesh['ctx'=32,'head'=8] {'ctx'}, dimensions={0} | all-to-all | bytes 524288 | tf_op jit(solution)/shard_map/all_to_all | solution.py:97
  274.4 3.9 %all-to-all-start.4 = ((f32[32,2,16,512]{3,2,1,0:T(8,128)}), f32[32,2,16,512]{3,2,1,0:T(8,128)S(1)}, u32[]{:S(2)}, u32[]{:S(2)}) async-start(f32[32,2,16,512]{3,2,1,0:T(8,128)} %bitcast.120), calls=%async_computation.4 | async-start | bytes 4194304 | tf_op jit(solution)/shard_map/all_to_all | solution.py:96
  281.8 24.4 %all-to-all-done.4 = f32[32,2,16,512]{3,2,1,0:T(8,128)S(1)} async-done(((f32[32,2,16,512]{3,2,1,0:T(8,128)}), f32[32,2,16,512]{3,2,1,0:T(8,128)S(1)}, u32[]{:S(2)}, u32[]{:S(2)}) %all-to-all-start.4) | async-done | bytes 2097184 | tf_op jit(solution)/shard_map/all_to_all | solution.py:96
  308.7 9.0 %scatter_fusion = f32[128,16,512]{2,1,0:T(8,128)} fusion(f32[128,16,512]{2,1,0:T(8,128)} %broadcast_in_dim.77, s32[64]{0:T(128)S(1)} %fusion.56, f32[64,16,512]{2,1,0:T(8,128)S(1)} %bitcast.117), kind=kCustom, calls=%fused_computation.2 | custom fusion | flops 524288 | bytes 6291712 | tf_op jit(solution)/shard_map/scatter-add | solution.py:103
  317.8 5.8 %copy.67 = f32[128,16,512]{0,1,2:T(8,128)} copy(f32[128,16,512]{2,1,0:T(8,128)} %scatter_fusion) | data formatting | bytes 8388608 | tf_op jit(solution)/shard_map/scatter-add | solution.py:103
  327.1 45.7 %reduce-scatter.3.cloned.1.call-done = f32[128,16,64]{0,1,2:T(8,128)} async-done(((f32[128,16,512]{0,1,2:T(8,128)}), f32[128,16,64]{0,1,2:T(8,128)}) %reduce-scatter.3.cloned.1.call-update) | async-done | bytes 524304 | tf_op jit(solution)/shard_map/reduce_scatter | solution.py:111
  (76 shorter events, 55.0 us)
Async XLA Ops:
  7.2 28.5 %copy-start = (bf16[128,1024]{1,0:T(8,128)(2,1)S(1)}, bf16[128,1024]{1,0:T(8,128)(2,1)}, u32[]{:S(2)}) copy-start(bf16[128,1024]{1,0:T(8,128)(2,1)} %param.13) | copy-start | bytes 786436
  24.4 11.3 %copy-start.6 = (s32[32,1,2]{2,1,0:T(1,128)}, s32[32,1,2]{2,1,0:T(1,128)S(1)}, u32[]{:S(2)}) copy-start(s32[32,1,2]{2,1,0:T(1,128)S(1)} %all_to_all.34) | copy-start | bytes 772
  27.2 56.6 %all-to-all-start = ((bf16[8,128,16,64]{1,3,2,0:T(8,128)(2,1)}), bf16[8,128,16,64]{1,3,2,0:T(8,128)(2,1)S(1)}, u32[]{:S(2)}, u32[]{:S(2)}) async-start(bf16[8,128,16,64]{1,3,2,0:T(8,128)(2,1)} %stack.2), calls=%async_computation | async-start | bytes 4194304 | tf_op jit(solution)/shard_map/all_to_all | solution.py:11
  83.8 16.8 %all-to-all-start.3 = ((bf16[32,2,1024]{2,1,0:T(2,128)(2,1)}), bf16[32,2,1024]{2,1,0:T(2,128)(2,1)S(1)}, u32[]{:S(2)}, u32[]{:S(2)}) async-start(bf16[32,2,1024]{2,1,0:T(2,128)(2,1)} %reshape.183), calls=%async_computation.3 | async-start | bytes 262144 | tf_op jit(solution)/shard_map/all_to_all | solution.py:34
  97.2 28.0 %copy-start.2 = (bf16[128,16,512]{2,1,0:T(8,128)(2,1)S(1)}, bf16[128,16,512]{2,1,0:T(8,128)(2,1)}, u32[]{:S(2)}) copy-start(bf16[128,16,512]{2,1,0:T(8,128)(2,1)} %param.14) | copy-start | bytes 6291460
  100.6 24.7 %all-to-all-start.2 = ((bf16[32,2,16,512]{3,2,1,0:T(8,128)(2,1)}), bf16[32,2,16,512]{3,2,1,0:T(8,128)(2,1)S(1)}, u32[]{:S(2)}, u32[]{:S(2)}) async-start(bf16[32,2,16,512]{3,2,1,0:T(8,128)(2,1)} %bitcast.119), calls=%async_computation.2 | async-start | bytes 2097152 | tf_op jit(solution)/shard_map/all_to_all | solution.py:33
  125.2 1.8 copy-start.4
  125.2 1.8 copy-start.3
  128.5 3.8 copy-start.1
  192.6 1.8 copy-start.4
  192.6 1.8 copy-start.3
  195.9 3.8 copy-start.1
  260.5 18.3 %copy-start.7 = (s32[32,1,2]{2,1,0:T(1,128)S(1)}, s32[32,1,2]{2,1,0:T(1,128)}, u32[]{:S(2)}) copy-start(s32[32,1,2]{2,1,0:T(1,128)} %copy-done.6) | copy-start | bytes 772
  274.4 31.9 %all-to-all-start.4 = ((f32[32,2,16,512]{3,2,1,0:T(8,128)}), f32[32,2,16,512]{3,2,1,0:T(8,128)S(1)}, u32[]{:S(2)}, u32[]{:S(2)}) async-start(f32[32,2,16,512]{3,2,1,0:T(8,128)} %bitcast.120), calls=%async_computation.4 | async-start | bytes 4194304 | tf_op jit(solution)/shard_map/all_to_all | solution.py:96
  278.3 47.4 %reduce-scatter.5.cloned.1.call-start = ((), (), s32[]{:S(2)}) async-start(), calls=%async_computation.9 | async-start | bytes 589824 | tf_op jit(solution)/shard_map/reduce_scatter | solution.py:112
  281.8 91.1 %reduce-scatter.3.cloned.1.call-start = ((), (), s32[]{:S(2)}) async-start(), calls=%async_computation.8 | async-start | bytes 4718592 | tf_op jit(solution)/shard_map/reduce_scatter | solution.py:111
  323.6 1.0 copy-start.5
Sparse Core Ops, SparseCore 0:
  281.9 29.2 reduce-scatter.4
  323.7 49.0 reduce-scatter.2
